TPU v7x, 512 devices: a whole 4x4x16 slice. The times are simulated.
512 devices in a mesh: wide: 64 (over z_hi, x, y), narrow: 8 (over z_lo, core).
Axes of the slice: x: 4, y: 4, z: 16 (z_hi: 4, z_lo: 4; z = z_hi * 4 + z_lo), core: 2. Of those that a mesh axis runs over, the one named last changes fastest.
Arguments:
- initial_state: float32 [33554432], P(('wide', 'narrow')), may hold values from -6 to 6
- angles: float32 [3, 25], replicated, may hold values from -3.140625 to 3.140625
- pairings: int32 [3, 25], replicated, may hold values from 0 to 24, each once within a row
Outputs:
- final_state: float32 [33554432], P(('wide', 'narrow'))
Inputs may be any that keep to these rules, and one draw needn't show every extreme that they name: Each row of pairings names every qubit once.
All inputs are finite; a program needn't handle non-finite values.
Results may differ from a plain program's by a relative error of at most 0.00025.
Values sent between devices are 32-bit elements; how exact they have to be, the bound alone decides.
No kernel may reach another device: no remote copies, remote signals or barrier semaphores. Data moves between devices by JAX's collectives and lax.ppermute only.
A program may use at most 64 MiB of HBM per device.

v0:
```python
import jax
import jax.numpy as jnp
from jax import lax
from jax.sharding import PartitionSpec as P


def from_partner(block, axis, bit):
    count = lax.axis_size(axis)
    route = []
    for low in range(count):
        high = low | 1 << bit
        if high != low and high < count:
            route += [(low, high), (high, low)]
    return lax.ppermute(block, axis, route)


def kron_rotation(angle_list):
    matrix = jnp.ones((1, 1), jnp.float32)
    for angle_value in angle_list:
        cosine = jnp.cos(angle_value / 2)
        sine_half = jnp.sin(angle_value / 2)
        single = jnp.stack([jnp.stack([cosine, -sine_half]), jnp.stack([sine_half, cosine])])
        matrix = jnp.kron(single, matrix)
    return matrix


def rotate_bits(amplitudes, layer_angles, bit_low, qubit_low, bit_count):
    amp_count = amplitudes.shape[0]
    for offset in range(0, bit_count, 7):
        group_bits = min(7, bit_count - offset)
        matrix = kron_rotation(
            [layer_angles[qubit_low + offset + member] for member in range(group_bits)]
        )
        group_size = 2**group_bits
        inner_size = 2 ** (bit_low + offset)
        outer_size = amp_count // (group_size * inner_size)
        if inner_size == 1:
            blocks = amplitudes.reshape(outer_size, group_size)
            amplitudes = jnp.dot(blocks, matrix.T, precision=lax.Precision.HIGHEST).reshape(
                amp_count
            )
        else:
            blocks = amplitudes.reshape(outer_size, group_size, inner_size)
            amplitudes = jnp.einsum(
                "ij,ajb->aib", matrix, blocks, precision=lax.Precision.HIGHEST
            ).reshape(amp_count)
    return amplitudes


def entangle(amplitudes, pair_row, positions):
    pair_count = pair_row.shape[0] // 2
    first_qubits = pair_row[0 : 2 * pair_count : 2]
    second_qubits = pair_row[1 : 2 * pair_count : 2]
    joint_bits = (
        jnp.right_shift(positions[None, :], first_qubits[:, None])
        & jnp.right_shift(positions[None, :], second_qubits[:, None])
        & 1
    )
    parity = jnp.sum(joint_bits, axis=0) % 2
    return jnp.where(parity == 1, -amplitudes, amplitudes)


def remap_narrow(arranged):
    return lax.all_to_all(arranged, "narrow", split_axis=1, concat_axis=1, tiled=True)


def shards(initial_state, angles, pairings):
    amplitudes = initial_state
    amp_count = amplitudes.shape[0]
    local_bits = amp_count.bit_length() - 1
    wide_size = lax.axis_size("wide")
    narrow_size = lax.axis_size("narrow")
    wide_bits = wide_size.bit_length() - 1
    narrow_bits = narrow_size.bit_length() - 1
    device_bits = wide_bits + narrow_bits
    low_bits = local_bits - device_bits
    wide_index = lax.axis_index("wide")
    device_number = wide_index * narrow_size + lax.axis_index("narrow")
    local_index = jnp.arange(amp_count, dtype=jnp.int32)
    plain_positions = device_number * amp_count + local_index
    for layer_number in range(angles.shape[0]):
        layer_angles = angles[layer_number]
        amplitudes = rotate_bits(amplitudes, layer_angles, 0, 0, local_bits)
        arranged = remap_narrow(amplitudes.reshape(wide_size, narrow_size, -1))
        moved = rotate_bits(
            arranged.reshape(amp_count), layer_angles, low_bits, local_bits, narrow_bits
        )
        amplitudes = remap_narrow(moved.reshape(wide_size, narrow_size, -1)).reshape(amp_count)
        for wide_bit in range(wide_bits):
            partner = from_partner(amplitudes, "wide", wide_bit)
            angle_value = layer_angles[local_bits + narrow_bits + wide_bit]
            cosine = jnp.cos(angle_value / 2)
            sine_half = jnp.sin(angle_value / 2)
            upper_bit = jnp.right_shift(wide_index, wide_bit) & 1
            factor = jnp.where(upper_bit == 1, sine_half, -sine_half)
            amplitudes = cosine * amplitudes + factor * partner
        amplitudes = entangle(amplitudes, pairings[layer_number], plain_positions)
    return amplitudes


def solution(mesh):
    return jax.shard_map(
        shards,
        mesh=mesh,
        in_specs=(P(("wide", "narrow")), P(), P()),
        out_specs=P(("wide", "narrow")),
        check_vma=False,
    )
```

profile of v0, /device:TPU:1, one launch (start us, length us, event | category | flops | bytes accessed | tf_op | source)
XLA Modules:
  0.0 410.0 jit_solution(11338411407731627635)
XLA Ops:
  0.0 2.1 fusion.20
  12.1 2.1 fusion.21
  22.8 10.3 %all-to-all-start = ((f32[64,8,128]{2,0,1:T(8,128)}), f32[64,8,128]{2,0,1:T(8,128)S(1)}, u32[]{:S(2)}, u32[]{:S(2)}) async-start(f32[64,8,128]{2,0,1:T(8,128)} %copy.44), calls=%async_computation | async-start | bytes 524288 | tf_op jit(solution)/shard_map/all_to_all | solution.py:64
  61.6 5.1 %all-to-all-start.1 = ((f32[64,8,128]{2,0,1:T(8,128)}), f32[64,8,128]{2,0,1:T(8,128)S(1)}, u32[]{:S(2)}, u32[]{:S(2)}) async-start(f32[64,8,128]{2,0,1:T(8,128)} %copy.46), calls=%async_computation.1 | async-start | bytes 524288 | tf_op jit(solution)/shard_map/all_to_all | solution.py:64
  66.9 5.8 %and_reduce_fusion.2 = (s32[65536]{0:T(1024)S(1)}, s32[65536]{0:T(1024)S(1)}, s32[65536]{0:T(1024)S(1)}) fusion(s32[12]{0:T(128)S(1)} %slice.407, s32[12]{0:T(128)S(1)} %slice.406, s32[65536]{0:T(1024)S(1)} %iota_add_fusion, s32[12]{0:T(128)S(1)} %slice.425, s32[12]{0:T(128)S(1)} %slice.424, s32[12]{0:T(128)S(1)} %slice.416, s32[12]{0:T(128)S(1)} %slice.415), kind=kLoop, calls=%fused_computation.5 | loop fusion | flops 11599872 | bytes 1048864 | tf_op jit(solution)/shard_map/reduce_sum | solution.py:59
  72.7 2.7 all-to-all-done.1
  75.6 1.9 collective-permute-start
  79.3 5.0 %collective-permute-done = f32[65536]{0:T(1024)S(1)} collective-permute-done((f32[65536]{0:T(1024)S(1)}, f32[65536]{0:T(1024)S(1)}, u32[]{:S(2)}, u32[]{:S(2)}) %collective-permute-start) | collective-permute-done | bytes 262176 | tf_op jit(solution)/shard_map/ppermute | solution.py:14
  84.4 2.2 collective-permute-start.1
  87.6 6.0 %collective-permute-done.1 = f32[65536]{0:T(1024)S(1)} collective-permute-done((f32[65536]{0:T(1024)S(1)}, f32[65536]{0:T(1024)S(1)}, u32[]{:S(2)}, u32[]{:S(2)}) %collective-permute-start.1) | collective-permute-done | bytes 262176 | tf_op jit(solution)/shard_map/ppermute | solution.py:14
  93.7 1.9 collective-permute-start.2
  97.3 3.4 collective-permute-done.2
  100.8 1.9 collective-permute-start.3
  103.9 5.5 %collective-permute-done.3 = f32[65536]{0:T(1024)S(1)} collective-permute-done((f32[65536]{0:T(1024)S(1)}, f32[65536]{0:T(1024)S(1)}, u32[]{:S(2)}, u32[]{:S(2)}) %collective-permute-start.3) | collective-permute-done | bytes 262176 | tf_op jit(solution)/shard_map/ppermute | solution.py:14
  109.5 6.0 %collective-permute-start.4 = (f32[65536]{0:T(1024)S(1)}, f32[65536]{0:T(1024)S(1)}, u32[]{:S(2)}, u32[]{:S(2)}) collective-permute-start(f32[65536]{0:T(1024)S(1)} %multiply_add_fusion.11), channel_id=1, source_target_pairs={{0,128},{128,0},{8,136},{136,8},{16,144},{144,16},{24,152},{152,24... | collective-permute-start | bytes 786440 | tf_op jit(solution)/shard_map/ppermute | solution.py:14
  117.1 22.9 %collective-permute-done.4 = f32[65536]{0:T(1024)S(1)} collective-permute-done((f32[65536]{0:T(1024)S(1)}, f32[65536]{0:T(1024)S(1)}, u32[]{:S(2)}, u32[]{:S(2)}) %collective-permute-start.4) | collective-permute-done | bytes 262176 | tf_op jit(solution)/shard_map/ppermute | solution.py:14
  140.0 15.7 %collective-permute-start.5 = (f32[65536]{0:T(1024)S(1)}, f32[65536]{0:T(1024)S(1)}, u32[]{:S(2)}, u32[]{:S(2)}) collective-permute-start(f32[65536]{0:T(1024)S(1)} %multiply_add_fusion.10), channel_id=1, source_target_pairs={{0,256},{256,0},{8,264},{264,8},{16,272},{272,16},{24,280},{280,24... | collective-permute-start | bytes 786440 | tf_op jit(solution)/shard_map/ppermute | solution.py:14
  157.1 12.7 %collective-permute-done.5 = f32[65536]{0:T(1024)S(1)} collective-permute-done((f32[65536]{0:T(1024)S(1)}, f32[65536]{0:T(1024)S(1)}, u32[]{:S(2)}, u32[]{:S(2)}) %collective-permute-start.5) | collective-permute-done | bytes 262176 | tf_op jit(solution)/shard_map/ppermute | solution.py:14
  172.5 3.8 all-to-all-start.2
  179.4 5.7 %all-to-all-done.2 = f32[64,8,128]{2,0,1:T(8,128)S(1)} async-done(((f32[64,8,128]{2,0,1:T(8,128)}), f32[64,8,128]{2,0,1:T(8,128)S(1)}, u32[]{:S(2)}, u32[]{:S(2)}) %all-to-all-start.2) | async-done | bytes 262176 | tf_op jit(solution)/shard_map/all_to_all | solution.py:64
  186.4 4.4 %all-to-all-start.3 = ((f32[64,8,128]{2,0,1:T(8,128)}), f32[64,8,128]{2,0,1:T(8,128)S(1)}, u32[]{:S(2)}, u32[]{:S(2)}) async-start(f32[64,8,128]{2,0,1:T(8,128)} %copy.52), calls=%async_computation.3 | async-start | bytes 524288 | tf_op jit(solution)/shard_map/all_to_all | solution.py:64
  192.9 6.6 %all-to-all-done.3 = f32[64,8,128]{2,0,1:T(8,128)S(1)} async-done(((f32[64,8,128]{2,0,1:T(8,128)}), f32[64,8,128]{2,0,1:T(8,128)S(1)}, u32[]{:S(2)}, u32[]{:S(2)}) %all-to-all-start.3) | async-done | bytes 262176 | tf_op jit(solution)/shard_map/all_to_all | solution.py:64
  199.6 3.2 collective-permute-start.6
  204.6 3.7 collective-permute-done.6
  208.4 4.8 %collective-permute-start.7 = (f32[65536]{0:T(1024)S(1)}, f32[65536]{0:T(1024)S(1)}, u32[]{:S(2)}, u32[]{:S(2)}) collective-permute-start(f32[65536]{0:T(1024)S(1)} %multiply_add_fusion.9), channel_id=1, source_target_pairs={{0,16},{16,0},{8,24},{24,8},{32,48},{48,32},{40,56},{56,40},{64,80... | collective-permute-start | bytes 786440 | tf_op jit(solution)/shard_map/ppermute | solution.py:14
  214.3 3.4 collective-permute-done.7
  217.7 3.1 collective-permute-start.8
  222.6 2.3 collective-permute-done.8
  224.9 4.7 %collective-permute-start.9 = (f32[65536]{0:T(1024)S(1)}, f32[65536]{0:T(1024)S(1)}, u32[]{:S(2)}, u32[]{:S(2)}) collective-permute-start(f32[65536]{0:T(1024)S(1)} %multiply_add_fusion.7), channel_id=1, source_target_pairs={{0,64},{64,0},{8,72},{72,8},{16,80},{80,16},{24,88},{88,24},{32,96... | collective-permute-start | bytes 786440 | tf_op jit(solution)/shard_map/ppermute | solution.py:14
  230.5 2.9 collective-permute-done.9
  233.5 7.3 %collective-permute-start.10 = (f32[65536]{0:T(1024)S(1)}, f32[65536]{0:T(1024)S(1)}, u32[]{:S(2)}, u32[]{:S(2)}) collective-permute-start(f32[65536]{0:T(1024)S(1)} %multiply_add_fusion.6), channel_id=1, source_target_pairs={{0,128},{128,0},{8,136},{136,8},{16,144},{144,16},{24,152},{152,24... | collective-permute-start | bytes 786440 | tf_op jit(solution)/shard_map/ppermute | solution.py:14
  244.2 18.3 %collective-permute-done.10 = f32[65536]{0:T(1024)S(1)} collective-permute-done((f32[65536]{0:T(1024)S(1)}, f32[65536]{0:T(1024)S(1)}, u32[]{:S(2)}, u32[]{:S(2)}) %collective-permute-start.10) | collective-permute-done | bytes 262176 | tf_op jit(solution)/shard_map/ppermute | solution.py:14
  262.6 10.6 %collective-permute-start.11 = (f32[65536]{0:T(1024)S(1)}, f32[65536]{0:T(1024)S(1)}, u32[]{:S(2)}, u32[]{:S(2)}) collective-permute-start(f32[65536]{0:T(1024)S(1)} %multiply_add_fusion.5), channel_id=1, source_target_pairs={{0,256},{256,0},{8,264},{264,8},{16,272},{272,16},{24,280},{280,24... | collective-permute-start | bytes 786440 | tf_op jit(solution)/shard_map/ppermute | solution.py:14
  273.4 19.7 %collective-permute-done.11 = f32[65536]{0:T(1024)S(1)} collective-permute-done((f32[65536]{0:T(1024)S(1)}, f32[65536]{0:T(1024)S(1)}, u32[]{:S(2)}, u32[]{:S(2)}) %collective-permute-start.11) | collective-permute-done | bytes 262176 | tf_op jit(solution)/shard_map/ppermute | solution.py:14
  295.9 3.8 all-to-all-start.4
  301.8 6.6 %all-to-all-done.4 = f32[64,8,128]{2,0,1:T(8,128)S(1)} async-done(((f32[64,8,128]{2,0,1:T(8,128)}), f32[64,8,128]{2,0,1:T(8,128)S(1)}, u32[]{:S(2)}, u32[]{:S(2)}) %all-to-all-start.4) | async-done | bytes 262176 | tf_op jit(solution)/shard_map/all_to_all | solution.py:64
  309.0 12.1 %all_to_all.30 = f32[64,8,128]{2,0,1:T(8,128)S(1)} all-to-all(f32[64,8,128]{2,0,1:T(8,128)S(1)} %copy.58), channel_id=1, replica_groups=mesh['wide'=64,'narrow'=8] {'narrow'}, dimensions={1} | all-to-all | bytes 524288 | tf_op jit(solution)/shard_map/all_to_all | solution.py:64
  321.3 3.2 collective-permute-start.12
  325.3 4.7 %collective-permute-done.12 = f32[65536]{0:T(1024)S(1)} collective-permute-done((f32[65536]{0:T(1024)S(1)}, f32[65536]{0:T(1024)S(1)}, u32[]{:S(2)}, u32[]{:S(2)}) %collective-permute-start.12) | collective-permute-done | bytes 262176 | tf_op jit(solution)/shard_map/ppermute | solution.py:14
  330.1 4.8 %collective-permute-start.13 = (f32[65536]{0:T(1024)S(1)}, f32[65536]{0:T(1024)S(1)}, u32[]{:S(2)}, u32[]{:S(2)}) collective-permute-start(f32[65536]{0:T(1024)S(1)} %multiply_add_fusion.4), channel_id=1, source_target_pairs={{0,16},{16,0},{8,24},{24,8},{32,48},{48,32},{40,56},{56,40},{64,80... | collective-permute-start | bytes 786440 | tf_op jit(solution)/shard_map/ppermute | solution.py:14
  335.7 3.6 collective-permute-done.13
  339.4 2.9 collective-permute-start.14
  343.1 3.4 collective-permute-done.14
  346.5 4.4 %collective-permute-start.15 = (f32[65536]{0:T(1024)S(1)}, f32[65536]{0:T(1024)S(1)}, u32[]{:S(2)}, u32[]{:S(2)}) collective-permute-start(f32[65536]{0:T(1024)S(1)} %multiply_add_fusion.2), channel_id=1, source_target_pairs={{0,64},{64,0},{8,72},{72,8},{16,80},{80,16},{24,88},{88,24},{32,96... | collective-permute-start | bytes 786440 | tf_op jit(solution)/shard_map/ppermute | solution.py:14
  351.6 3.5 collective-permute-done.15
  357.9 26.5 %collective-permute-done.16 = f32[65536]{0:T(1024)S(1)} collective-permute-done((f32[65536]{0:T(1024)S(1)}, f32[65536]{0:T(1024)S(1)}, u32[]{:S(2)}, u32[]{:S(2)}) %collective-permute-start.16) | collective-permute-done | bytes 262176 | tf_op jit(solution)/shard_map/ppermute | solution.py:14
  384.5 13.2 %collective-permute-start.17 = (f32[65536]{0:T(1024)S(1)}, f32[65536]{0:T(1024)S(1)}, u32[]{:S(2)}, u32[]{:S(2)}) collective-permute-start(f32[65536]{0:T(1024)S(1)} %multiply_add_fusion), channel_id=1, source_target_pairs={{0,256},{256,0},{8,264},{264,8},{16,272},{272,16},{24,280},{280,24... | collective-permute-start | bytes 786440 | tf_op jit(solution)/shard_map/ppermute | solution.py:14
  398.5 10.6 %collective-permute-done.17 = f32[65536]{0:T(1024)S(1)} collective-permute-done((f32[65536]{0:T(1024)S(1)}, f32[65536]{0:T(1024)S(1)}, u32[]{:S(2)}, u32[]{:S(2)}) %collective-permute-start.17) | collective-permute-done | bytes 262176 | tf_op jit(solution)/shard_map/ppermute | solution.py:14
  (267 shorter events, 29.9 us)
Async XLA Ops:
  0.0 19.9 %copy-start = (f32[65536]{0:T(1024)S(1)}, f32[65536]{0:T(1024)}, u32[]{:S(2)}) copy-start(f32[65536]{0:T(1024)} %param.3) | copy-start | bytes 786436
  22.8 12.8 %copy-start.1 = (f32[3,25]{1,0:T(4,128)S(1)}, f32[3,25]{1,0:T(4,128)}, u32[]{:S(2)}) copy-start(f32[3,25]{1,0:T(4,128)} %param.4) | copy-start | bytes 904
  22.8 37.5 %all-to-all-start = ((f32[64,8,128]{2,0,1:T(8,128)}), f32[64,8,128]{2,0,1:T(8,128)S(1)}, u32[]{:S(2)}, u32[]{:S(2)}) async-start(f32[64,8,128]{2,0,1:T(8,128)} %copy.44), calls=%async_computation | async-start | bytes 524288 | tf_op jit(solution)/shard_map/all_to_all | solution.py:64
  33.1 22.7 %copy-start.2 = (s32[3,25]{1,0:T(4,128)S(1)}, s32[3,25]{1,0:T(4,128)}, u32[]{:S(2)}) copy-start(s32[3,25]{1,0:T(4,128)} %param.5) | copy-start | bytes 904
  61.6 13.8 %all-to-all-start.1 = ((f32[64,8,128]{2,0,1:T(8,128)}), f32[64,8,128]{2,0,1:T(8,128)S(1)}, u32[]{:S(2)}, u32[]{:S(2)}) async-start(f32[64,8,128]{2,0,1:T(8,128)} %copy.46), calls=%async_computation.1 | async-start | bytes 524288 | tf_op jit(solution)/shard_map/all_to_all | solution.py:64
  75.6 8.7 %collective-permute-start = (f32[65536]{0:T(1024)S(1)}, f32[65536]{0:T(1024)S(1)}, u32[]{:S(2)}, u32[]{:S(2)}) collective-permute-start(f32[65536]{0:T(1024)S(1)} %bitcast.536), channel_id=1, source_target_pairs={{0,8},{8,0},{16,24},{24,16},{32,40},{40,32},{48,56},{56,48},{64,72... | collective-permute-start | bytes 786440 | tf_op jit(solution)/shard_map/ppermute | solution.py:14
  84.4 9.2 %collective-permute-start.1 = (f32[65536]{0:T(1024)S(1)}, f32[65536]{0:T(1024)S(1)}, u32[]{:S(2)}, u32[]{:S(2)}) collective-permute-start(f32[65536]{0:T(1024)S(1)} %multiply_add_fusion.14), channel_id=1, source_target_pairs={{0,16},{16,0},{8,24},{24,8},{32,48},{48,32},{40,56},{56,40},{64,80... | collective-permute-start | bytes 786440 | tf_op jit(solution)/shard_map/ppermute | solution.py:14
  93.7 7.1 %collective-permute-start.2 = (f32[65536]{0:T(1024)S(1)}, f32[65536]{0:T(1024)S(1)}, u32[]{:S(2)}, u32[]{:S(2)}) collective-permute-start(f32[65536]{0:T(1024)S(1)} %multiply_add_fusion.13), channel_id=1, source_target_pairs={{0,32},{32,0},{8,40},{40,8},{16,48},{48,16},{24,56},{56,24},{64,96... | collective-permute-start | bytes 786440 | tf_op jit(solution)/shard_map/ppermute | solution.py:14
  100.8 8.6 %collective-permute-start.3 = (f32[65536]{0:T(1024)S(1)}, f32[65536]{0:T(1024)S(1)}, u32[]{:S(2)}, u32[]{:S(2)}) collective-permute-start(f32[65536]{0:T(1024)S(1)} %multiply_add_fusion.12), channel_id=1, source_target_pairs={{0,64},{64,0},{8,72},{72,8},{16,80},{80,16},{24,88},{88,24},{32,96... | collective-permute-start | bytes 786440 | tf_op jit(solution)/shard_map/ppermute | solution.py:14
  109.5 30.5 %collective-permute-start.4 = (f32[65536]{0:T(1024)S(1)}, f32[65536]{0:T(1024)S(1)}, u32[]{:S(2)}, u32[]{:S(2)}) collective-permute-start(f32[65536]{0:T(1024)S(1)} %multiply_add_fusion.11), channel_id=1, source_target_pairs={{0,128},{128,0},{8,136},{136,8},{16,144},{144,16},{24,152},{152,24... | collective-permute-start | bytes 786440 | tf_op jit(solution)/shard_map/ppermute | solution.py:14
  140.0 29.8 %collective-permute-start.5 = (f32[65536]{0:T(1024)S(1)}, f32[65536]{0:T(1024)S(1)}, u32[]{:S(2)}, u32[]{:S(2)}) collective-permute-start(f32[65536]{0:T(1024)S(1)} %multiply_add_fusion.10), channel_id=1, source_target_pairs={{0,256},{256,0},{8,264},{264,8},{16,272},{272,16},{24,280},{280,24... | collective-permute-start | bytes 786440 | tf_op jit(solution)/shard_map/ppermute | solution.py:14
  172.5 12.6 %all-to-all-start.2 = ((f32[64,8,128]{2,0,1:T(8,128)}), f32[64,8,128]{2,0,1:T(8,128)S(1)}, u32[]{:S(2)}, u32[]{:S(2)}) async-start(f32[64,8,128]{2,0,1:T(8,128)} %copy.50), calls=%async_computation.2 | async-start | bytes 524288 | tf_op jit(solution)/shard_map/all_to_all | solution.py:64
  186.4 13.1 %all-to-all-start.3 = ((f32[64,8,128]{2,0,1:T(8,128)}), f32[64,8,128]{2,0,1:T(8,128)S(1)}, u32[]{:S(2)}, u32[]{:S(2)}) async-start(f32[64,8,128]{2,0,1:T(8,128)} %copy.52), calls=%async_computation.3 | async-start | bytes 524288 | tf_op jit(solution)/shard_map/all_to_all | solution.py:64
  199.6 8.7 %collective-permute-start.6 = (f32[65536]{0:T(1024)S(1)}, f32[65536]{0:T(1024)S(1)}, u32[]{:S(2)}, u32[]{:S(2)}) collective-permute-start(f32[65536]{0:T(1024)S(1)} %bitcast.537), channel_id=1, source_target_pairs={{0,8},{8,0},{16,24},{24,16},{32,40},{40,32},{48,56},{56,48},{64,72... | collective-permute-start | bytes 786440 | tf_op jit(solution)/shard_map/ppermute | solution.py:14
  208.4 9.2 %collective-permute-start.7 = (f32[65536]{0:T(1024)S(1)}, f32[65536]{0:T(1024)S(1)}, u32[]{:S(2)}, u32[]{:S(2)}) collective-permute-start(f32[65536]{0:T(1024)S(1)} %multiply_add_fusion.9), channel_id=1, source_target_pairs={{0,16},{16,0},{8,24},{24,8},{32,48},{48,32},{40,56},{56,40},{64,80... | collective-permute-start | bytes 786440 | tf_op jit(solution)/shard_map/ppermute | solution.py:14
  217.7 7.1 %collective-permute-start.8 = (f32[65536]{0:T(1024)S(1)}, f32[65536]{0:T(1024)S(1)}, u32[]{:S(2)}, u32[]{:S(2)}) collective-permute-start(f32[65536]{0:T(1024)S(1)} %multiply_add_fusion.8), channel_id=1, source_target_pairs={{0,32},{32,0},{8,40},{40,8},{16,48},{48,16},{24,56},{56,24},{64,96... | collective-permute-start | bytes 786440 | tf_op jit(solution)/shard_map/ppermute | solution.py:14
  224.9 8.6 %collective-permute-start.9 = (f32[65536]{0:T(1024)S(1)}, f32[65536]{0:T(1024)S(1)}, u32[]{:S(2)}, u32[]{:S(2)}) collective-permute-start(f32[65536]{0:T(1024)S(1)} %multiply_add_fusion.7), channel_id=1, source_target_pairs={{0,64},{64,0},{8,72},{72,8},{16,80},{80,16},{24,88},{88,24},{32,96... | collective-permute-start | bytes 786440 | tf_op jit(solution)/shard_map/ppermute | solution.py:14
  233.5 29.0 %collective-permute-start.10 = (f32[65536]{0:T(1024)S(1)}, f32[65536]{0:T(1024)S(1)}, u32[]{:S(2)}, u32[]{:S(2)}) collective-permute-start(f32[65536]{0:T(1024)S(1)} %multiply_add_fusion.6), channel_id=1, source_target_pairs={{0,128},{128,0},{8,136},{136,8},{16,144},{144,16},{24,152},{152,24... | collective-permute-start | bytes 786440 | tf_op jit(solution)/shard_map/ppermute | solution.py:14
  262.6 30.5 %collective-permute-start.11 = (f32[65536]{0:T(1024)S(1)}, f32[65536]{0:T(1024)S(1)}, u32[]{:S(2)}, u32[]{:S(2)}) collective-permute-start(f32[65536]{0:T(1024)S(1)} %multiply_add_fusion.5), channel_id=1, source_target_pairs={{0,256},{256,0},{8,264},{264,8},{16,272},{272,16},{24,280},{280,24... | collective-permute-start | bytes 786440 | tf_op jit(solution)/shard_map/ppermute | solution.py:14
  295.9 12.5 %all-to-all-start.4 = ((f32[64,8,128]{2,0,1:T(8,128)}), f32[64,8,128]{2,0,1:T(8,128)S(1)}, u32[]{:S(2)}, u32[]{:S(2)}) async-start(f32[64,8,128]{2,0,1:T(8,128)} %copy.56), calls=%async_computation.4 | async-start | bytes 524288 | tf_op jit(solution)/shard_map/all_to_all | solution.py:64
  321.3 8.7 %collective-permute-start.12 = (f32[65536]{0:T(1024)S(1)}, f32[65536]{0:T(1024)S(1)}, u32[]{:S(2)}, u32[]{:S(2)}) collective-permute-start(f32[65536]{0:T(1024)S(1)} %bitcast.538), channel_id=1, source_target_pairs={{0,8},{8,0},{16,24},{24,16},{32,40},{40,32},{48,56},{56,48},{64,72... | collective-permute-start | bytes 786440 | tf_op jit(solution)/shard_map/ppermute | solution.py:14
  330.1 9.2 %collective-permute-start.13 = (f32[65536]{0:T(1024)S(1)}, f32[65536]{0:T(1024)S(1)}, u32[]{:S(2)}, u32[]{:S(2)}) collective-permute-start(f32[65536]{0:T(1024)S(1)} %multiply_add_fusion.4), channel_id=1, source_target_pairs={{0,16},{16,0},{8,24},{24,8},{32,48},{48,32},{40,56},{56,40},{64,80... | collective-permute-start | bytes 786440 | tf_op jit(solution)/shard_map/ppermute | solution.py:14
  339.4 7.1 %collective-permute-start.14 = (f32[65536]{0:T(1024)S(1)}, f32[65536]{0:T(1024)S(1)}, u32[]{:S(2)}, u32[]{:S(2)}) collective-permute-start(f32[65536]{0:T(1024)S(1)} %multiply_add_fusion.3), channel_id=1, source_target_pairs={{0,32},{32,0},{8,40},{40,8},{16,48},{48,16},{24,56},{56,24},{64,96... | collective-permute-start | bytes 786440 | tf_op jit(solution)/shard_map/ppermute | solution.py:14
  346.5 8.6 %collective-permute-start.15 = (f32[65536]{0:T(1024)S(1)}, f32[65536]{0:T(1024)S(1)}, u32[]{:S(2)}, u32[]{:S(2)}) collective-permute-start(f32[65536]{0:T(1024)S(1)} %multiply_add_fusion.2), channel_id=1, source_target_pairs={{0,64},{64,0},{8,72},{72,8},{16,80},{80,16},{24,88},{88,24},{32,96... | collective-permute-start | bytes 786440 | tf_op jit(solution)/shard_map/ppermute | solution.py:14
  355.2 29.3 %collective-permute-start.16 = (f32[65536]{0:T(1024)S(1)}, f32[65536]{0:T(1024)S(1)}, u32[]{:S(2)}, u32[]{:S(2)}) collective-permute-start(f32[65536]{0:T(1024)S(1)} %multiply_add_fusion.1), channel_id=1, source_target_pairs={{0,128},{128,0},{8,136},{136,8},{16,144},{144,16},{24,152},{152,24... | collective-permute-start | bytes 786440 | tf_op jit(solution)/shard_map/ppermute | solution.py:14
  384.5 24.7 %collective-permute-start.17 = (f32[65536]{0:T(1024)S(1)}, f32[65536]{0:T(1024)S(1)}, u32[]{:S(2)}, u32[]{:S(2)}) collective-permute-start(f32[65536]{0:T(1024)S(1)} %multiply_add_fusion), channel_id=1, source_target_pairs={{0,256},{256,0},{8,264},{264,8},{16,272},{272,16},{24,280},{280,24... | collective-permute-start | bytes 786440 | tf_op jit(solution)/shard_map/ppermute | solution.py:14
where the time goes:
time: 412 us; the launch traced here: 410 us
  waiting for transfers between devices  180 us (44%)
  starting transfers between devices  121 us (29%)
  between operations  58.9 us (14%)
  other arithmetic  16.4 us (4%)
  local copies, waits for them, and re-layouts  15.5 us (4%)
  blocking collectives  12.1 us (3%)
  matrix products  5.98 us (1%)
    ppermute x18, waiting for transfers between devices, from_partner(): return lax.ppermute(block, axis, route)  158 us
    ppermute x18, starting transfers between devices, from_partner(): return lax.ppermute(block, axis, route)  93.7 us
    all_to_all x5, starting transfers between devices, remap_narrow(): lax.all_to_all(arranged, 'narrow', split_axis=1, concat_axis=1, tiled=True)  27.4 us
    all_to_all x5, waiting for transfers between devices, remap_narrow(): lax.all_to_all(arranged, 'narrow', split_axis=1, concat_axis=1, tiled=True)  21.6 us
    all_to_all x1, blocking collectives, remap_narrow(): lax.all_to_all(arranged, 'narrow', split_axis=1, concat_axis=1, tiled=True)  12.1 us
  transfers between devices with their start and end apart: 23, of which 22 were waited for; matrix products, arithmetic and copies ran while one was open for 4% of the time, Pallas kernels for 0%

commit v1 on v0

v1 whole, which is shorter than its diff:
```python
import jax
import jax.numpy as jnp
from jax import lax
from jax.experimental import pallas as pl
from jax.experimental.pallas import tpu as pltpu
from jax.sharding import PartitionSpec as P

SIDE = 256
LANES = 128
CORE = 16
PAIRS = 12
AXES = ("wide", "narrow")


def trig(angle):
    t = angle * 0.5
    u = t * t
    sine = 1.0 / 6227020800
    for term in (-1.0 / 39916800, 1.0 / 362880, -1.0 / 5040, 1.0 / 120, -1.0 / 6, 1.0):
        sine = sine * u + term
    cosine = -1.0 / 87178291200
    for term in (1.0 / 479001600, -1.0 / 3628800, 1.0 / 40320, -1.0 / 720, 1.0 / 24, -0.5, 1.0):
        cosine = cosine * u + term
    return cosine, sine * t


def iota(shape, axis):
    return lax.broadcasted_iota(jnp.int32, shape, axis)


def choose(pairings):
    bad = jnp.int32(0)
    hot = jnp.int32(0)
    one = jnp.int32(1)
    for k in range(PAIRS):
        p, r = pairings[1, 2 * k], pairings[1, 2 * k + 1]
        p_bit, r_bit = lax.shift_left(one, p), lax.shift_left(one, r)
        bad = bad | jnp.where(p > CORE, r_bit, 0) | jnp.where(r > CORE, p_bit, 0)
        hot = hot | jnp.where(p == CORE, r_bit, 0) | jnp.where(r == CORE, p_bit, 0)
    free = ~bad & 255
    trades = []
    for position in range(8, 16):
        calm = free & ~hot
        pool = jnp.where(calm != 0, calm, free)
        taken = jnp.where(((bad >> position) & 1) == 1, pool & -pool, 0)
        free = free & ~taken
        trades.append(taken)
    for position in range(8, 16):
        calm = free & ~hot
        taken = jnp.where(((hot >> position) & 1) == 1, calm & -calm, 0)
        free = free & ~taken
        trades[position - 8] = trades[position - 8] | taken
    left = jnp.int32(0)
    for position in range(8, 16):
        taken = trades[position - 8]
        stays = jnp.where(taken == 0, lax.shift_left(one, jnp.int32(position)), taken)
        left = left | (stays & hot)
    return trades, jnp.where(left != 0, 1, 0)


def qubits_at(trades):
    table = []
    for column in range(8):
        held = jnp.int32(column)
        for position in range(8, 16):
            held = jnp.where(trades[position - 8] == 1 << column, position, held)
        table.append(held)
    for position in range(8, 16):
        taken = trades[position - 8]
        held = jnp.int32(0)
        for column in range(1, 8):
            held = held + jnp.where(taken >= 1 << column, 1, 0)
        table.append(jnp.where(taken == 0, position, held))
    return table


def angle_table(entries):
    place = iota((8, LANES), 0) * LANES + iota((8, LANES), 1)
    table = jnp.zeros((8, LANES), jnp.float32)
    for row, lane, value in entries:
        table = jnp.where(place == row * LANES + lane, value, table)
    return table


def bit_masks():
    i, j = iota((LANES, LANES), 0), iota((LANES, LANES), 1)
    same = [((i ^ j) >> b) & 1 == 0 for b in range(7)]
    upper = [(i >> b) & 1 == 1 for b in range(7)]
    return same, upper


def kron_matrix(masks, cosines, sines, row, base, transposed):
    same, upper = masks
    total = None
    for b in range(7):
        c = cosines[row : row + 1, base + b : base + b + 1]
        s = sines[row : row + 1, base + b : base + b + 1]
        if transposed:
            s = -s
        factor = jnp.where(same[b], c, jnp.where(upper[b], s, -s))
        total = factor if total is None else total * factor
    c = cosines[row : row + 1, base + 7 : base + 8]
    s = sines[row : row + 1, base + 7 : base + 8]
    if transposed:
        s = -s
    top = jnp.concatenate([total * c, total * -s], axis=1)
    low = jnp.concatenate([total * s, total * c], axis=1)
    return jnp.concatenate([top, low], axis=0)


def parts(value):
    high = value.astype(jnp.bfloat16)
    low = (value - high.astype(jnp.float32)).astype(jnp.bfloat16)
    return high, low


def product(left, right):
    (lh, ll), (rh, rl) = left, right

    def dot(a, b):
        return jnp.dot(a, b, preferred_element_type=jnp.float32)

    return dot(lh, rh) + (dot(lh, rl) + dot(ll, rh))


def load_matrix(ref):
    return jnp.concatenate(
        [ref[pl.ds(0, SIDE, stride=2), :], ref[pl.ds(1, SIDE, stride=2), :]], axis=1
    )


def store_matrix(ref, value):
    ref[pl.ds(0, SIDE, stride=2), :] = value[:, :LANES]
    ref[pl.ds(1, SIDE, stride=2), :] = value[:, LANES:]


def trade_bits(work, trades):
    lane = iota((SIDE, LANES), 1)
    row = iota((SIDE, LANES), 0)
    for bit in range(8):
        taken = trades[bit]
        step = 1 << bit
        row_up = (row & step) != 0

        @pl.when((taken != 0) & (taken < LANES))
        def _():
            lane_up = (lane & taken) != 0
            for half in range(2):
                columns = slice(half * LANES, half * LANES + LANES)
                held = work[:, columns]
                later = pltpu.roll(held, SIDE - step, 0)
                sooner = pltpu.roll(held, step, 0)
                from_later = pltpu.roll(later, taken, 1)
                from_sooner = pltpu.roll(sooner, LANES - taken, 1)
                moved = jnp.where(lane_up, from_later, from_sooner)
                work[:, columns] = jnp.where(row_up == lane_up, held, moved)

        @pl.when(taken == LANES)
        def _():
            first = work[:, :LANES]
            second = work[:, LANES:]
            work[:, :LANES] = jnp.where(row_up, pltpu.roll(second, step, 0), first)
            work[:, LANES:] = jnp.where(row_up, second, pltpu.roll(first, SIDE - step, 0))


def first_kernel(angles, pairings, state, out, work):
    table = angle_table([(0, q, angles[0, q]) for q in range(16)])
    cosines, sines = trig(table)
    masks = bit_masks()
    rows = parts(kron_matrix(masks, cosines, sines, 0, 8, False))
    columns = parts(kron_matrix(masks, cosines, sines, 0, 0, True))
    value = load_matrix(state)
    value = product(rows, parts(value))
    work[...] = product(parts(value), columns)
    trades, _ = choose(pairings)
    trade_bits(work, trades)
    store_matrix(out, work[...])


def signs(index, pairings, layer, place, keep=None):
    parity = jnp.zeros(index.shape, jnp.int32)
    for k in range(PAIRS):
        p, r = place(pairings[layer, 2 * k]), place(pairings[layer, 2 * k + 1])
        if keep is not None:
            p = jnp.where(keep(p, r), p, 31)
        parity = parity ^ (lax.shift_right_logical(index, p) & lax.shift_right_logical(index, r))
    return 1.0 - 2.0 * (parity & 1).astype(jnp.float32)


CHIP_1, CHIP_2, COLUMN_2, CHIP_3, ROW_2, ROW_3, COLUMN_3 = range(7)
MINE_1, OTHER_1, MINE_2, OTHER_2, MINE_LATE, OTHER_LATE, LAST = range(7)


def prepare_kernel(angles, pairings, high, low, sign, coefficients, flag, places):
    trades, needed = choose(pairings)
    flag[0] = needed
    held = qubits_at(trades)
    for position in range(16):
        places[position] = held[position]
    for position in range(16, 25):
        places[position] = jnp.int32(position)
    entries = []
    for layer in range(3):
        entries += [(layer, p, angles[layer, held[p]]) for p in range(16)]
        entries += [(layer, p, angles[layer, p]) for p in range(16, 25)]
    cosines, sines = trig(angle_table(entries))
    masks = bit_masks()
    for slot, layer, base, transposed in (
        (CHIP_1, 0, 17, False),
        (CHIP_2, 1, 17, False),
        (COLUMN_2, 1, 0, True),
        (CHIP_3, 2, 17, False),
        (ROW_2, 1, 8, False),
        (ROW_3, 2, 8, False),
        (COLUMN_3, 2, 0, True),
    ):
        high[slot], low[slot] = parts(
            kron_matrix(masks, cosines, sines, layer, base, transposed)
        )
    wide, narrow = lax.axis_index("wide"), lax.axis_index("narrow")
    chip = wide * 4 + lax.shift_right_logical(narrow, 1)
    core = narrow & 1
    turn = jnp.where(core == 1, sines, -sines)
    coefficients[0:8, :] = cosines
    coefficients[8:16, :] = turn
    local = iota((SIDE, SIDE), 0) * SIDE + iota((SIDE, SIDE), 1) + lax.shift_left(chip, 17)
    mine = local + lax.shift_left(core, 16)
    other = local + lax.shift_left(1 - core, 16)

    def outer(q):
        return places[q]

    def inner(q):
        place = places[q]
        moved = jnp.where(place > CORE, place - 9, place + 9)
        return jnp.where((place < 8) | (place == CORE), place, moved)

    def in_rows(place):
        return (place >= 8) & (place < 16)

    def late(p, r):
        return in_rows(p) | in_rows(r)

    def early(p, r):
        return (p <= CORE) & (r <= CORE)

    sign[MINE_1] = signs(mine, pairings, 0, inner)
    sign[OTHER_1] = signs(other, pairings, 0, inner)
    sign[MINE_2] = signs(mine, pairings, 1, inner, early)
    sign[OTHER_2] = signs(other, pairings, 1, inner, early)
    sign[MINE_LATE] = signs(mine, pairings, 1, outer, late)
    sign[OTHER_LATE] = signs(other, pairings, 1, outer, late)
    sign[LAST] = signs(mine, pairings, 2, outer)


def core_turn(coefficients, layer):
    c = coefficients[layer : layer + 1, CORE : CORE + 1]
    s = coefficients[8 + layer : 9 + layer, CORE : CORE + 1]
    return c, s


def second_kernel(flag, mine_ref, other_ref, high, low, sign, coefficients, out, spare):
    def matrix(slot):
        return high[slot], low[slot]

    mine = product(matrix(CHIP_1), parts(load_matrix(mine_ref)))
    other = product(matrix(CHIP_1), parts(load_matrix(other_ref)))
    c, s = core_turn(coefficients, 0)
    mine, other = c * mine + s * other, c * other - s * mine
    mine, other = mine * sign[MINE_1], other * sign[OTHER_1]
    c, s = core_turn(coefficients, 1)
    mine, other = c * mine + s * other, c * other - s * mine
    mine = product(matrix(CHIP_2), parts(mine))
    other = product(matrix(CHIP_2), parts(other))
    mine = product(parts(mine), matrix(COLUMN_2)) * sign[MINE_2]
    other = product(parts(other), matrix(COLUMN_2)) * sign[OTHER_2]
    c, s = core_turn(coefficients, 2)
    waits = jnp.full((1, 1), flag[0], jnp.int32) == 1
    c, s = jnp.where(waits, 1.0, c), jnp.where(waits, 0.0, s)
    mine = c * mine + s * other
    store_matrix(out, product(matrix(CHIP_3), parts(mine)))


def third_kernel(pairings, flag, mine_ref, other_ref, high, low, sign, coefficients, out, work):
    def matrix(slot):
        return high[slot], low[slot]

    trades, _ = choose(pairings)
    mine = product(matrix(ROW_2), parts(load_matrix(mine_ref)))
    work[...] = mine * sign[MINE_LATE]

    @pl.when(flag[0] == 1)
    def _():
        other = product(matrix(ROW_2), parts(load_matrix(other_ref))) * sign[OTHER_LATE]
        c, s = core_turn(coefficients, 2)
        work[...] = c * work[...] + s * other

    mine = product(matrix(ROW_3), parts(work[...]))
    mine = product(parts(mine), matrix(COLUMN_3))
    work[...] = mine * sign[LAST]
    trade_bits(work, trades)
    store_matrix(out, work[...])


def call(kernel, in_spaces, out_shapes, scratch, flops):
    specs = [pl.BlockSpec(memory_space=space) for space in in_spaces]
    outs = [jax.ShapeDtypeStruct(shape, dtype) for shape, dtype, _ in out_shapes]
    out_specs = [pl.BlockSpec(memory_space=space) for _, _, space in out_shapes]
    return pl.pallas_call(
        kernel,
        in_specs=specs,
        out_shape=outs,
        out_specs=out_specs,
        scratch_shapes=scratch,
        compiler_params=pltpu.CompilerParams(vmem_limit_bytes=40 * 1024 * 1024),
        cost_estimate=pl.CostEstimate(flops=flops, bytes_accessed=4_000_000, transcendentals=0),
    )


def shards(initial_state, angles, pairings):
    V, S = pltpu.VMEM, pltpu.SMEM
    devices = lax.axis_size("wide") * lax.axis_size("narrow")
    chips = [list(range(core, devices, 2)) for core in range(2)]
    rows = 2 * SIDE
    flat = ((rows, LANES), jnp.float32, V)
    work = [pltpu.VMEM((SIDE, SIDE), jnp.float32)]
    product_flops = 3 * 2 * SIDE**3

    def across(value):
        value = value.reshape(SIDE, SIDE)
        value = lax.all_to_all(value, AXES, 0, 0, tiled=True, axis_index_groups=chips)
        return value.reshape(rows, LANES)

    def beside(value):
        return lax.ppermute(value, AXES, [(d, d ^ 1) for d in range(devices)])

    state = initial_state.reshape(rows, LANES)
    (state,) = call(first_kernel, [S, S, V], [flat], work, 2 * product_flops)(
        angles, pairings, state
    )
    state = across(state)
    high, low, sign, coefficients, flag = call(
        prepare_kernel,
        [S, S],
        [
            ((7, SIDE, SIDE), jnp.bfloat16, V),
            ((7, SIDE, SIDE), jnp.bfloat16, V),
            ((7, SIDE, SIDE), jnp.float32, V),
            ((16, LANES), jnp.float32, V),
            ((1,), jnp.int32, S),
        ],
        [pltpu.SMEM((25,), jnp.int32)],
        product_flops,
    )(angles, pairings)
    (state,) = call(second_kernel, [S, V, V, V, V, V, V], [flat], work, 7 * product_flops)(
        flag, state, beside(state), high, low, sign, coefficients
    )
    state = across(state)
    other = lax.cond(flag[0] == 1, beside, lambda value: value, state)
    (state,) = call(third_kernel, [S, S, V, V, V, V, V, V], [flat], work, 3 * product_flops)(
        pairings, flag, state, other, high, low, sign, coefficients
    )
    return state.reshape(-1)


def solution(mesh):
    return jax.shard_map(
        shards,
        mesh=mesh,
        in_specs=(P(AXES), P(), P()),
        out_specs=P(AXES),
        check_vma=False,
    )
```

time: 412 us -> 108 us (0.26)
  waiting for transfers between devices: 180 us -> 23 us
  starting transfers between devices: 121 us -> 19.8 us
  between operations: 58.9 us -> 0.7 us
  blocking collectives: 12.1 us -> 46 us
  other arithmetic: 16.4 us -> 0 us
  Pallas kernels: 0 us -> 15 us
  local copies, waits for them, and re-layouts: 15.5 us -> 3.5 us
  matrix products: 5.98 us -> 0 us
    ppermute x18 -> x2, waiting for transfers between devices: 158 us -> 1.27 us  [beside(): return lax.ppermute(value, AXES, [(d, d ^ 1) for d in range(devices)])]
    ppermute x18 -> x2, starting transfers between devices: 93.7 us -> 10.6 us  [beside(): return lax.ppermute(value, AXES, [(d, d ^ 1) for d in range(devices)])]
    all_to_all x1, blocking collectives: 12.1 us -> 46 us  [across(): lax.all_to_all(value, AXES, 0, 0, tiled=True, axis_index_groups=chips)]
    all_to_all x5 -> x1, starting transfers between devices: 27.4 us -> 9.17 us  [across(): lax.all_to_all(value, AXES, 0, 0, tiled=True, axis_index_groups=chips)]
    pallas_call x0 -> x4, Pallas kernels: none -> 15 us  [the longest x1 5.76 us: shards(): call(prepare_kernel, [S, S], [((7, SIDE, SIDE), jnp.bfloat16, V), ((7, SI...]
    slice x10 -> x0, local copies, waits for them, and re-layouts: 6.18 us -> none  [the longest x4 5.6 us: shards(): angle_value = layer_angles[local_bits + narrow_bits + wide_bit]]
    dot_general x12 -> x0, matrix products: 5.98 us -> none  [the longest x9 4.83 us: rotate_bits(): jnp.einsum('ij,ajb->aib', matrix, blocks, precision=lax.Precision.HIGHEST)]
    reduce_sum x1 -> x0, other arithmetic: 5.85 us -> none  [entangle(): parity = jnp.sum(joint_bits, axis=0) % 2]
  transfers between devices with their start and end apart: 23 -> 3, of which waited for: 22 -> 2; matrix products, arithmetic and copies ran while one was open for 4% -> 0% of each run, Pallas kernels for 0% -> 5%
where the time goes in v1:
time: 108 us
  blocking collectives  46 us (43%)
  waiting for transfers between devices  23 us (21%)
  starting transfers between devices  19.8 us (18%)
  Pallas kernels  15 us (14%)
  local copies, waits for them, and re-layouts  3.5 us (3%)
    all_to_all x1, blocking collectives, across(): lax.all_to_all(value, AXES, 0, 0, tiled=True, axis_index_groups=chips)  46 us
    all_to_all x1, waiting for transfers between devices, across(): lax.all_to_all(value, AXES, 0, 0, tiled=True, axis_index_groups=chips)  21.7 us
    ppermute x2, starting transfers between devices, beside(): return lax.ppermute(value, AXES, [(d, d ^ 1) for d in range(devices)])  10.6 us
    all_to_all x1, starting transfers between devices, across(): lax.all_to_all(value, AXES, 0, 0, tiled=True, axis_index_groups=chips)  9.17 us
    pallas_call x1, Pallas kernels, shards(): call(prepare_kernel, [S, S], [((7, SIDE, SIDE), jnp.bfloat16, V), ((7, SI...  5.76 us
    pallas_call x1, Pallas kernels, shards(): call(third_kernel, [S, S, V, V, V, V, V, V], [flat], work, 3 * product_fl...  4.18 us
    unnamed x12, local copies, waits for them, and re-layouts  3.5 us
    pallas_call x1, Pallas kernels, shards(): call(second_kernel, [S, V, V, V, V, V, V], [flat], work, 7 * product_flops)  2.9 us
  transfers between devices with their start and end apart: 3, of which 2 were waited for; matrix products, arithmetic and copies ran while one was open for 0% of the time, Pallas kernels for 5%

profile of v1, /device:TPU:1, one launch (start us, length us, event | category | flops | bytes accessed | tf_op | source)
XLA Modules:
  0.0 108.0 jit_solution(11638966003420062797)
XLA Ops:
  0.0 0.0 copy-start.2
  0.0 0.7 copy-done.2
  0.7 0.0 copy-start.4
  0.7 0.9 copy-done.4
  1.6 0.0 copy-start.5
  1.6 0.7 copy-done.5
  2.3 2.2 %shard_map.38 = f32[512,128]{1,0:T(8,128)S(1)} custom-call(f32[3,25]{1,0:T(4,128)S(1)} %copy-done.5, s32[3,25]{1,0:T(4,128)S(1)} %copy-done.2, f32[512,128]{1,0:T(8,128)S(1)} %bitcast.10), custom_call_target="tpu_custom_call" | custom-call | flops 201326592 | bytes 4000000 | tf_op jit(solution)/shard_map/pallas_call | solution.py:338
  4.5 46.0 %all_to_all.18 = f32[256,1,256]{2,1,0:T(1,128)S(1)} all-to-all(f32[256,1,256]{2,1,0:T(1,128)S(1)} %bitcast.9), channel_id=1, replica_groups={{0,2,4,6,8,10,12,14,16,18,20,22,24,26,28,30,32,34,36,38,40,42,44,46,48,..., dimensions={0} | all-to-all | bytes 524288 | tf_op jit(solution)/shard_map/all_to_all | solution.py:331
  50.5 6.1 %collective-permute-start.1 = (f32[512,128]{1,0:T(8,128)S(1)}, f32[512,128]{1,0:T(8,128)S(1)}, u32[]{:S(2)}, u32[]{:S(2)}) collective-permute-start(f32[512,128]{1,0:T(8,128)S(1)} %bitcast.7), channel_id=1, source_target_pairs={{0,1},{1,0},{2,3},{3,2},{4,5},{5,4},{6,7},{7,6},{8,9},{9,8},{10,11... | collective-permute-start | bytes 786440 | tf_op jit(solution)/shard_map/ppermute | solution.py:335
  56.7 5.8 %shard_map.37 = (bf16[7,256,256]{2,1,0:T(8,128)(2,1)S(1)}, bf16[7,256,256]{2,1,0:T(8,128)(2,1)S(1)}, f32[7,256,256]{2,1,0:T(8,128)S(1)}, f32[16,128]{1,0:T(8,128)S(1)}, s32[1]{0:T(128)}) custom-call(f32[3,25]{1,0:T(4,128)S(1)} %copy-done.5, s32[3,25]{1,0:T(4,128)S(1)} %copy-done.2), custom_call_target="tpu_custom_call" | custom-call | flops 100663296 | bytes 4000000 | tf_op jit(solution)/shard_map/pallas_call | solution.py:342
  62.4 0.0 copy-start
  62.4 0.0 collective-permute-done.1.other_ref
  62.5 0.0 copy-start.3
  62.5 2.9 %shard_map.39 = f32[512,128]{1,0:T(8,128)} custom-call(s32[1]{0:T(128)} %get-tuple-element.15.flag, f32[512,128]{1,0:T(8,128)S(1)} %bitcast.8, f32[512,128]{1,0:T(8,128)S(1)} %collective-permute-done.1.other_ref, bf16[7,256,256]{2,1,0:T(8,128)(2,1)S(1)} %get-tuple-element.16.high, bf16[7,256,256]{2,1,0:T(8,128)(2,1)S(1)} %get-tuple-element.17.low, ...), custom_call_target="tpu_custom_call" | custom-call | flops 704643072 | bytes 4000000 | tf_op jit(solution)/shard_map/pallas_call | solution.py:355
  65.4 0.0 copy-done
  65.4 9.2 %all-to-all-start.1 = ((f32[256,1,256]{2,1,0:T(1,128)}), f32[256,1,256]{2,1,0:T(1,128)S(1)}, u32[]{:S(2)}, u32[]{:S(2)}) async-start(f32[256,1,256]{2,1,0:T(1,128)} %bitcast.3), calls=%async_computation.1 | async-start | bytes 524288 | tf_op jit(solution)/shard_map/all_to_all | solution.py:331
  75.2 21.7 %all-to-all-done.1 = f32[256,1,256]{2,1,0:T(1,128)S(1)} async-done(((f32[256,1,256]{2,1,0:T(1,128)}), f32[256,1,256]{2,1,0:T(1,128)S(1)}, u32[]{:S(2)}, u32[]{:S(2)}) %all-to-all-start.1) | async-done | bytes 262176 | tf_op jit(solution)/shard_map/all_to_all | solution.py:331
  96.9 5.7 %conditional.1 = (f32[512,128]{1,0:T(8,128)}) conditional(s32[]{:T(128)} %bitcast.5, f32[512,128]{1,0:T(8,128)S(1)} %bitcast.11, f32[512,128]{1,0:T(8,128)S(1)} %bitcast.12), branch_computations={%region_0.0_spmd, %region_1.0_spmd} | conditional | bytes 1048624 | solution.py:359
  96.9 4.5 %collective-permute-start = (f32[512,128]{1,0:T(8,128)S(1)}, f32[512,128]{1,0:T(8,128)}, u32[]{:S(2)}, u32[]{:S(2)}) collective-permute-start(f32[512,128]{1,0:T(8,128)S(1)} %param.1), channel_id=1, source_target_pairs={{0,1},{1,0},{2,3},{3,2},{4,5},{5,4},{6,7},{7,6},{8,9},{9,8},{10,11... | collective-permute-start | bytes 786440 | tf_op jit(solution)/shard_map/cond/branch_1_fun/ppermute | solution.py:335
  101.4 1.3 %collective-permute-done = f32[512,128]{1,0:T(8,128)} collective-permute-done((f32[512,128]{1,0:T(8,128)S(1)}, f32[512,128]{1,0:T(8,128)}, u32[]{:S(2)}, u32[]{:S(2)}) %collective-permute-start) | collective-permute-done | bytes 262176 | tf_op jit(solution)/shard_map/cond/branch_1_fun/ppermute | solution.py:335
  102.6 0.0 copy-done.3
  102.6 0.0 copy-start.1
  102.6 1.2 %copy-done.1 = bf16[7,256,256]{2,1,0:T(8,128)(2,1)S(1)} copy-done((bf16[7,256,256]{2,1,0:T(8,128)(2,1)S(1)}, bf16[7,256,256]{2,1,0:T(8,128)(2,1)}, u32[]{:S(2)}) %copy-start.1) | copy-done | bytes 917528
  103.8 4.2 %shard_map.40 = f32[512,128]{1,0:T(8,128)} custom-call(s32[3,25]{1,0:T(4,128)S(1)} %copy-done.3, s32[1]{0:T(128)} %get-tuple-element.15.flag, f32[512,128]{1,0:T(8,128)S(1)} %bitcast.13, f32[512,128]{1,0:T(8,128)} %get-tuple-element.20.other_ref, bf16[7,256,256]{2,1,0:T(8,128)(2,1)S(1)} %get-tuple-element.16.high, bf16[7,256,256]{2,1,0:T(8,128)(2,1)S(1)} %copy-done.1, ...), custom_call_target="tpu_custom_call" | custom-call | flops 301989888 | bytes 4000000 | tf_op jit(solution)/shard_map/pallas_call | solution.py:360
Async XLA Ops:
  0.0 0.7 copy-start.2
  0.7 0.9 copy-start.4
  1.6 0.7 copy-start.5
  50.5 11.9 %collective-permute-start.1 = (f32[512,128]{1,0:T(8,128)S(1)}, f32[512,128]{1,0:T(8,128)S(1)}, u32[]{:S(2)}, u32[]{:S(2)}) collective-permute-start(f32[512,128]{1,0:T(8,128)S(1)} %bitcast.7), channel_id=1, source_target_pairs={{0,1},{1,0},{2,3},{3,2},{4,5},{5,4},{6,7},{7,6},{8,9},{9,8},{10,11... | collective-permute-start | bytes 786440 | tf_op jit(solution)/shard_map/ppermute | solution.py:335
  62.4 2.9 %copy-start = (bf16[7,256,256]{2,1,0:T(8,128)(2,1)}, bf16[7,256,256]{2,1,0:T(8,128)(2,1)S(1)}, u32[]{:S(2)}) copy-start(bf16[7,256,256]{2,1,0:T(8,128)(2,1)S(1)} %get-tuple-element.17.low) | copy-start | bytes 2752516
  62.5 40.2 %copy-start.3 = (s32[3,25]{1,0:T(4,128)S(1)}, s32[3,25]{1,0:T(4,128)}, u32[]{:S(2)}) copy-start(s32[3,25]{1,0:T(4,128)} %pairings.5) | copy-start | bytes 904
  65.4 31.5 %all-to-all-start.1 = ((f32[256,1,256]{2,1,0:T(1,128)}), f32[256,1,256]{2,1,0:T(1,128)S(1)}, u32[]{:S(2)}, u32[]{:S(2)}) async-start(f32[256,1,256]{2,1,0:T(1,128)} %bitcast.3), calls=%async_computation.1 | async-start | bytes 524288 | tf_op jit(solution)/shard_map/all_to_all | solution.py:331
  96.9 5.7 %collective-permute-start = (f32[512,128]{1,0:T(8,128)S(1)}, f32[512,128]{1,0:T(8,128)}, u32[]{:S(2)}, u32[]{:S(2)}) collective-permute-start(f32[512,128]{1,0:T(8,128)S(1)} %param.1), channel_id=1, source_target_pairs={{0,1},{1,0},{2,3},{3,2},{4,5},{5,4},{6,7},{7,6},{8,9},{9,8},{10,11... | collective-permute-start | bytes 786440 | tf_op jit(solution)/shard_map/cond/branch_1_fun/ppermute | solution.py:335
  102.6 1.2 %copy-start.1 = (bf16[7,256,256]{2,1,0:T(8,128)(2,1)S(1)}, bf16[7,256,256]{2,1,0:T(8,128)(2,1)}, u32[]{:S(2)}) copy-start(bf16[7,256,256]{2,1,0:T(8,128)(2,1)} %copy-done) | copy-start | bytes 2752516
